TPU v7x, 512 devices: a whole 4x8x8 slice. The times are simulated.
512 devices in a mesh: row: 16 (over z_lo, x), col: 8 (over y), fiber: 4 (over z_hi, core).
Axes of the slice: x: 4, y: 8, z: 8 (z_hi: 2, z_lo: 4; z = z_hi * 4 + z_lo), core: 2. Of those that a mesh axis runs over, the one named last changes fastest.
Arguments:
- values: float32 [12288, 12288], P('row', ('col', 'fiber')), may hold values from -6 to 6
- tile_mask: int32 [96, 96], P('row', ('col', 'fiber')), may hold values from 0 to 1, as said below
- keep_mask: int32 [96, 96], P('row', ('col', 'fiber')), may hold values 0 or 1
Outputs:
- flows: float32 [12288, 12288], P('row', ('col', 'fiber'))
Inputs may be any that keep to these rules, and one draw needn't show every extreme that they name: `tile_mask`: 1 marks a tile that holds entries; every diagonal tile is 1, and tiles with low indices are denser.
All inputs are finite; a program needn't handle non-finite values. No bound on the sum of `keep_mask` on one device may be relied on, other than what follows from the above.
Results may differ from a plain program's by a relative error of at most 0.017.
Values may be sent and summed in bfloat16 or wider, within the bound.
No kernel may reach another device: no remote copies, remote signals or barrier semaphores. Data moves between devices by JAX's collectives and lax.ppermute only.
A program may use at most 64 MiB of HBM per device.

v0:
```python
import jax
import jax.numpy as jnp
from jax import lax
from jax.sharding import PartitionSpec as P


def cut_along(shard, dim, peers):
    lengths = shard.shape
    parts = shard.reshape(*lengths[:dim], peers, lengths[dim] // peers, *lengths[dim + 1 :])
    return jnp.moveaxis(parts, dim, 0)


def sum_at_owner(shard, axis, dim):
    parts = cut_along(shard, dim, lax.axis_size(axis))
    arrived = lax.all_to_all(parts, axis, split_axis=0, concat_axis=0, tiled=True)
    return arrived.astype(jnp.float32).sum(axis=0)


def sent_to_all(shard, axis):
    copies = jnp.broadcast_to(shard, (lax.axis_size(axis), *shard.shape))
    return lax.all_to_all(copies, axis, split_axis=0, concat_axis=0, tiled=True)


def taken_together(shard, axis):
    return sent_to_all(shard, axis).sum(axis=0)


def spread_tiles(mask, tile_size):
    count_rows, count_cols = mask.shape
    wide = jnp.broadcast_to(
        mask.astype(jnp.float32)[:, None, :, None], (count_rows, tile_size, count_cols, tile_size)
    )
    return wide.reshape(count_rows * tile_size, count_cols * tile_size)


def local(values, tile_mask, keep_mask):
    n_row = lax.axis_size("row")
    n_fib = lax.axis_size("fiber")
    tile_size = values.shape[1] // tile_mask.shape[1]
    weighted = (values * spread_tiles(tile_mask, tile_size)).astype(jnp.bfloat16)
    rows_dev, unit_width = weighted.shape
    sub_width = unit_width // n_fib
    unit_count = rows_dev // unit_width
    left_stack = weighted.reshape(rows_dev, n_fib, sub_width)
    right_stack = weighted.reshape(unit_count, n_fib, sub_width, unit_width)
    left_recv, right_recv = (
        lax.all_to_all(left_stack, "fiber", split_axis=1, concat_axis=1, tiled=True),
        lax.all_to_all(right_stack, "fiber", split_axis=1, concat_axis=1, tiled=True),
    )
    left_local = left_recv.reshape(rows_dev, unit_width)
    right_local = jnp.transpose(right_recv, (0, 2, 1, 3)).reshape(
        unit_count * sub_width, n_fib * unit_width
    )
    left_all = lax.all_gather(left_local, "col", axis=1, tiled=True)
    partial_product = jnp.dot(
        left_all,
        lax.all_gather(right_local, "row", axis=0, tiled=True),
        preferred_element_type=jnp.float32,
    )
    expanded = sum_at_owner(partial_product.astype(jnp.bfloat16), "fiber", 1)
    squared = expanded * expanded
    col_total = taken_together(jnp.sum(squared, axis=0), "row")
    col_scale = col_total / (rows_dev * n_row) + 1e-06
    return spread_tiles(keep_mask, tile_size) * squared / col_scale[None, :]


def solution(mesh):
    return jax.shard_map(
        local,
        mesh=mesh,
        in_specs=(
            P("row", ("col", "fiber")),
            P("row", ("col", "fiber")),
            P("row", ("col", "fiber")),
        ),
        out_specs=P("row", ("col", "fiber")),
        check_vma=False,
    )
```

profile of v0, /device:TPU:8, one launch (start us, length us, event | category | flops | bytes accessed | tf_op | source)
XLA Modules:
  0.0 311.7 jit_solution(8198016643156649648)
XLA Ops:
  6.5 0.7 convert_element_type.16
  7.2 1.6 copy.27
  8.9 0.2 broadcast_in_dim.7
  9.0 0.4 fusion
  9.4 30.0 %all_to_all.21 = bf16[768,4,96]{0,2,1:T(8,128)(2,1)} all-to-all(bf16[768,4,96]{0,2,1:T(8,128)(2,1)S(1)} %bitcast.34), channel_id=1, replica_groups=mesh['row'=16,'col'=8,'fiber'=4] {'fiber'}, dimensions={1} | all-to-all | bytes 1179648 | tf_op jit(solution)/shard_map/all_to_all | solution.py:47
  39.4 0.3 copy.28
  39.8 22.0 %all_to_all.22 = bf16[2,4,96,384]{3,2,0,1:T(8,128)(2,1)S(1)} all-to-all(bf16[2,4,96,384]{3,2,0,1:T(8,128)(2,1)S(1)} %copy.29), channel_id=1, replica_groups=mesh['row'=16,'col'=8,'fiber'=4] {'fiber'}, dimensions={1} | all-to-all | bytes 1179648 | tf_op jit(solution)/shard_map/all_to_all | solution.py:48
  61.9 0.5 copy.30
  62.3 0.9 copy.40
  63.2 34.8 %all-gather.3.cloned.1.call-done = bf16[768,3072]{0,1:T(8,128)(2,1)} async-done(((bf16[768,384]{0,1:T(8,128)(2,1)}), bf16[768,3072]{0,1:T(8,128)(2,1)}) %all-gather.3.cloned.1.call-update) | async-done | bytes 4718608 | tf_op jit(solution)/shard_map/all_gather | solution.py:54
  98.0 118.6 %all-gather.5.cloned.1.call-done = bf16[3072,1536]{1,0:T(8,128)(2,1)} async-done(((bf16[192,1536]{1,0:T(8,128)(2,1)}), bf16[3072,1536]{1,0:T(8,128)(2,1)}) %all-gather.5.cloned.1.call-update) | async-done | bytes 9437200 | tf_op jit(solution)/shard_map/all_gather | solution.py:57
  216.6 11.6 %convolution_convert_fusion = bf16[768,1536]{1,0:T(8,128)(2,1)S(1)} fusion(bf16[768,3072]{0,1:T(8,128)(2,1)} %all-gather.3.cloned.1.call-done, bf16[3072,1536]{1,0:T(8,128)(2,1)} %all-gather.5.cloned.1.call-done), kind=kOutput, calls=%fused_computation.1 | convolution fusion | flops 7248936960 | bytes 16515072 | tf_op jit(solution)/shard_map/dot_general | solution.py:55
  228.2 0.2 copy.44
  228.5 61.1 %all_to_all.23 = bf16[4,768,384]{2,1,0:T(8,128)(2,1)S(1)} all-to-all(bf16[4,768,384]{2,1,0:T(8,128)(2,1)S(1)} %bitcast.31), channel_id=1, replica_groups=mesh['row'=16,'col'=8,'fiber'=4] {'fiber'}, dimensions={0} | all-to-all | bytes 4718592 | tf_op jit(solution)/shard_map/all_to_all | solution.py:15
  289.6 0.4 convert_reduce_fusion
  289.9 0.1 multiply_reduce_fusion
  290.1 0.6 broadcast_in_dim.8
  290.7 4.1 %all-to-all-start.3 = ((f32[16,1,384]{2,1,0:T(1,128)}), f32[16,1,384]{2,1,0:T(1,128)}, u32[]{:S(2)}, u32[]{:S(2)}) async-start(f32[16,1,384]{2,1,0:T(1,128)} %broadcast_in_dim.8), calls=%async_computation.3 | async-start | bytes 49152 | tf_op jit(solution)/shard_map/all_to_all | solution.py:21
  294.9 0.2 broadcast_in_dim.6
  295.0 0.3 copy.45
  295.3 0.4 copy.33
  295.7 7.3 %all-to-all-done.3 = f32[16,1,384]{2,1,0:T(1,128)} async-done(((f32[16,1,384]{2,1,0:T(1,128)}), f32[16,1,384]{2,1,0:T(1,128)}, u32[]{:S(2)}, u32[]{:S(2)}) %all-to-all-start.3) | async-done | bytes 24608 | tf_op jit(solution)/shard_map/all_to_all | solution.py:21
  302.9 0.8 reduce_sum.29
  303.7 1.1 multiply_divide_fusion
  (9 shorter events, 0.2 us)
Async XLA Ops:
  6.5 91.5 %all-gather.3.cloned.1.call-start = ((), (), s32[]{:S(2)}) async-start(), calls=%async_computation.4 | async-start | bytes 5308416 | tf_op jit(solution)/shard_map/all_gather | solution.py:54
  39.4 177.2 %all-gather.5.cloned.1.call-start = ((), (), s32[]{:S(2)}) async-start(), calls=%async_computation.5 | async-start | bytes 10027008 | tf_op jit(solution)/shard_map/all_gather | solution.py:57
  289.6 5.3 %copy-start = (s32[6,3]{0,1:T(4,128)S(1)}, s32[6,3]{0,1:T(4,128)}, u32[]{:S(2)}) copy-start(s32[6,3]{0,1:T(4,128)} %param.5) | copy-start | bytes 220
  290.7 12.2 %all-to-all-start.3 = ((f32[16,1,384]{2,1,0:T(1,128)}), f32[16,1,384]{2,1,0:T(1,128)}, u32[]{:S(2)}, u32[]{:S(2)}) async-start(f32[16,1,384]{2,1,0:T(1,128)} %broadcast_in_dim.8), calls=%async_computation.3 | async-start | bytes 49152 | tf_op jit(solution)/shard_map/all_to_all | solution.py:21
Sparse Core Ops, SparseCore 0:
  39.5 58.4 all-gather.2
  100.1 116.4 all-gather.4
where the time goes:
time: 312 us
  waiting for transfers between devices  161 us (52%)
  blocking collectives  113 us (36%)
  between operations  13.5 us (4%)
  matrix products  11.6 us (4%)
  local copies, waits for them, and re-layouts  5.17 us (2%)
  starting transfers between devices  4.18 us (1%)
  other arithmetic  3.47 us (1%)
    all_gather x1, waiting for transfers between devices, local(): lax.all_gather(right_local, 'row', axis=0, tiled=True)  119 us
    all_to_all x1, blocking collectives, sum_at_owner(): lax.all_to_all(parts, axis, split_axis=0, concat_axis=0, tiled=True)  61.1 us
    all_gather x1, waiting for transfers between devices, local(): left_all = lax.all_gather(left_local, 'col', axis=1, tiled=True)  34.8 us
    all_to_all x1, blocking collectives, local(): lax.all_to_all(left_stack, 'fiber', split_axis=1, concat_axis=1, tiled=True)  30 us
    all_to_all x1, blocking collectives, local(): lax.all_to_all(right_stack, 'fiber', split_axis=1, concat_axis=1, tiled=T...  22 us
    dot_general x1, matrix products, local(): jnp.dot(left_all, lax.all_gather(right_local, 'row', axis=0, tiled=True),...  11.6 us
    all_to_all x1, waiting for transfers between devices, sent_to_all(): return lax.all_to_all(copies, axis, split_axis=0, concat_axis=0, tiled=True)  7.26 us
  transfers between devices with their start and end apart: 3, of which 3 were waited for; matrix products, arithmetic and copies ran while one was open for 1% of the time, Pallas kernels for 0%

commit v1 on v0

--- a/solution.py
+++ b/solution.py
@@ -51,7 +51,22 @@
     right_local = jnp.transpose(right_recv, (0, 2, 1, 3)).reshape(
         unit_count * sub_width, n_fib * unit_width
     )
-    left_all = lax.all_gather(left_local, "col", axis=1, tiled=True)
+    ways, here, step = (lax.axis_size("col"), lax.axis_index("col"), left_local.shape[1])
+    shape = [n * ways if d == 1 else n for d, n in enumerate(left_local.shape)]
+    left_all = lax.dynamic_update_slice_in_dim(
+        jnp.zeros(shape, left_local.dtype), left_local, here * step, axis=1
+    )
+    going_up = going_down = left_local
+    for far in range(1, ways // 2 + 1):
+        going_up = lax.ppermute(going_up, "col", [(d, (d + 1) % ways) for d in range(ways)])
+        left_all = lax.dynamic_update_slice_in_dim(
+            left_all, going_up, (here - far) % ways * step, axis=1
+        )
+        if 2 * far < ways:
+            going_down = lax.ppermute(going_down, "col", [(d, (d - 1) % ways) for d in range(ways)])
+            left_all = lax.dynamic_update_slice_in_dim(
+                left_all, going_down, (here + far) % ways * step, axis=1
+            )
     partial_product = jnp.dot(
         left_all,
         lax.all_gather(right_local, "row", axis=0, tiled=True),

time: 312 us -> 255 us (0.82)
  the two profiles are of different devices: /device:TPU:8 before, /device:TPU:56 now
where the time goes in v1:
time: 255 us; the launch traced here: 254 us
  blocking collectives  96.5 us (38%)
  waiting for transfers between devices  76 us (30%)
  starting transfers between devices  38.1 us (15%)
  local copies, waits for them, and re-layouts  14.7 us (6%)
  between operations  13.7 us (5%)
  matrix products  11.6 us (5%)
  other arithmetic  3.47 us (1%)
    all_to_all x1, blocking collectives, sum_at_owner(): lax.all_to_all(parts, axis, split_axis=0, concat_axis=0, tiled=True)  49.2 us
    all_gather x1, waiting for transfers between devices, local(): lax.all_gather(right_local, 'row', axis=0, tiled=True)  42.8 us
    all_to_all x1, blocking collectives, local(): lax.all_to_all(right_stack, 'fiber', split_axis=1, concat_axis=1, tiled=T...  29.9 us
    ppermute x4, waiting for transfers between devices, local(): lax.ppermute(going_up, 'col', [(d, (d + 1) % ways) for d in range(ways)])  25.9 us
    all_to_all x1, blocking collectives, local(): lax.all_to_all(left_stack, 'fiber', split_axis=1, concat_axis=1, tiled=True)  17.4 us
    ppermute x4, starting transfers between devices, local(): lax.ppermute(going_up, 'col', [(d, (d + 1) % ways) for d in range(ways)])  15.8 us
    all_to_all x1, starting transfers between devices, sent_to_all(): return lax.all_to_all(copies, axis, split_axis=0, concat_axis=0, tiled=True)  14.2 us
    dot_general x1, matrix products, local(): jnp.dot(left_all, lax.all_gather(right_local, 'row', axis=0, tiled=True),...  11.6 us
  transfers between devices with their start and end apart: 9, of which 6 were waited for; matrix products, arithmetic and copies ran while one was open for 4% of the time, Pallas kernels for 0%

profile of v1, /device:TPU:56, one launch (start us, length us, event | category | flops | bytes accessed | tf_op | source)
XLA Modules:
  0.0 254.1 jit_solution(12724763408935176923)
XLA Ops:
  7.2 1.6 copy.27
  9.8 29.9 %all_to_all.21 = bf16[2,4,96,384]{3,2,0,1:T(8,128)(2,1)S(1)} all-to-all(bf16[2,4,96,384]{3,2,0,1:T(8,128)(2,1)S(1)} %copy.29), channel_id=1, replica_groups=mesh['row'=16,'col'=8,'fiber'=4] {'fiber'}, dimensions={1} | all-to-all | bytes 1179648 | tf_op jit(solution)/shard_map/all_to_all | solution.py:48
  40.1 0.9 copy.40
  41.0 17.4 %all_to_all.22 = bf16[768,4,96]{0,2,1:T(8,128)(2,1)S(1)} all-to-all(bf16[768,4,96]{0,2,1:T(8,128)(2,1)S(1)} %bitcast.34), channel_id=1, replica_groups=mesh['row'=16,'col'=8,'fiber'=4] {'fiber'}, dimensions={1} | all-to-all | bytes 1179648 | tf_op jit(solution)/shard_map/all_to_all | solution.py:47
  58.4 2.1 collective-permute-start
  60.5 3.8 %collective-permute-start.1 = (bf16[768,384]{0,1:T(8,128)(2,1)S(1)}, bf16[768,384]{0,1:T(8,128)(2,1)S(1)}, u32[]{:S(2)}, u32[]{:S(2)}) collective-permute-start(bf16[768,384]{0,1:T(8,128)(2,1)S(1)} %bitcast.39), channel_id=1, source_target_pairs={{0,28},{4,0},{8,4},{12,8},{16,12},{20,16},{24,20},{28,24},{1,29},{... | collective-permute-start | bytes 1769480 | tf_op jit(solution)/shard_map/ppermute | solution.py:66
  64.3 9.6 %collective-permute-done = bf16[768,384]{0,1:T(8,128)(2,1)S(1)} collective-permute-done((bf16[768,384]{0,1:T(8,128)(2,1)S(1)}, bf16[768,384]{0,1:T(8,128)(2,1)S(1)}, u32[]{:S(2)}, u32[]{:S(2)}) %collective-permute-start) | collective-permute-done | bytes 589856 | tf_op jit(solution)/shard_map/ppermute | solution.py:61
  73.8 3.4 %collective-permute-start.2 = (bf16[768,384]{0,1:T(8,128)(2,1)S(1)}, bf16[768,384]{0,1:T(8,128)(2,1)S(1)}, u32[]{:S(2)}, u32[]{:S(2)}) collective-permute-start(bf16[768,384]{0,1:T(8,128)(2,1)S(1)} %collective-permute-done), channel_id=1, source_target_pairs={{0,4},{4,8},{8,12},{12,16},{16,20},{20,24},{24,28},{28,0},{1,5},{5... | collective-permute-start | bytes 1769480 | tf_op jit(solution)/shard_map/ppermute | solution.py:61
  77.3 2.4 collective-permute-start.3
  79.7 8.8 %collective-permute-done.2 = bf16[768,384]{0,1:T(8,128)(2,1)S(1)} collective-permute-done((bf16[768,384]{0,1:T(8,128)(2,1)S(1)}, bf16[768,384]{0,1:T(8,128)(2,1)S(1)}, u32[]{:S(2)}, u32[]{:S(2)}) %collective-permute-start.2) | collective-permute-done | bytes 589856 | tf_op jit(solution)/shard_map/ppermute | solution.py:61
  88.5 4.7 %collective-permute-start.4 = (bf16[768,384]{0,1:T(8,128)(2,1)S(1)}, bf16[768,384]{0,1:T(8,128)(2,1)S(1)}, u32[]{:S(2)}, u32[]{:S(2)}) collective-permute-start(bf16[768,384]{0,1:T(8,128)(2,1)S(1)} %collective-permute-done.2), channel_id=1, source_target_pairs={{0,4},{4,8},{8,12},{12,16},{16,20},{20,24},{24,28},{28,0},{1,5},{5... | collective-permute-start | bytes 1769480 | tf_op jit(solution)/shard_map/ppermute | solution.py:61
  93.3 2.6 %broadcast_in_dim.9 = bf16[768,3072]{0,1:T(8,128)(2,1)} broadcast(bf16[]{:T(256)} %constant.54.clone.1), dimensions={} | broadcast | bytes 4718594 | tf_op jit(solution)/shard_map/broadcast_in_dim | solution.py:57
  96.7 1.9 collective-permute-start.5
  98.7 0.9 constant_dynamic-update-slice_fusion.6
  99.6 3.2 %collective-permute-done.4 = bf16[768,384]{0,1:T(8,128)(2,1)S(1)} collective-permute-done((bf16[768,384]{0,1:T(8,128)(2,1)S(1)}, bf16[768,384]{0,1:T(8,128)(2,1)S(1)}, u32[]{:S(2)}, u32[]{:S(2)}) %collective-permute-start.4) | collective-permute-done | bytes 589856 | tf_op jit(solution)/shard_map/ppermute | solution.py:61
  102.7 5.6 %collective-permute-start.6 = (bf16[768,384]{0,1:T(8,128)(2,1)S(1)}, bf16[768,384]{0,1:T(8,128)(2,1)S(1)}, u32[]{:S(2)}, u32[]{:S(2)}) collective-permute-start(bf16[768,384]{0,1:T(8,128)(2,1)S(1)} %collective-permute-done.4), channel_id=1, source_target_pairs={{0,4},{4,8},{8,12},{12,16},{16,20},{20,24},{24,28},{28,0},{1,5},{5... | collective-permute-start | bytes 1769480 | tf_op jit(solution)/shard_map/ppermute | solution.py:61
  109.2 0.9 constant_dynamic-update-slice_fusion.4
  112.7 4.4 %collective-permute-done.6 = bf16[768,384]{0,1:T(8,128)(2,1)S(1)} collective-permute-done((bf16[768,384]{0,1:T(8,128)(2,1)S(1)}, bf16[768,384]{0,1:T(8,128)(2,1)S(1)}, u32[]{:S(2)}, u32[]{:S(2)}) %collective-permute-start.6) | collective-permute-done | bytes 589856 | tf_op jit(solution)/shard_map/ppermute | solution.py:61
  117.9 42.8 %all-gather.2.cloned.1.call-done = bf16[3072,1536]{1,0:T(8,128)(2,1)} async-done(((bf16[192,1536]{1,0:T(8,128)(2,1)}), bf16[3072,1536]{1,0:T(8,128)(2,1)}) %all-gather.2.cloned.1.call-update) | async-done | bytes 9437200 | tf_op jit(solution)/shard_map/all_gather | solution.py:72
  160.7 11.6 %convolution_convert_fusion = bf16[768,1536]{1,0:T(8,128)(2,1)S(1)} fusion(bf16[768,3072]{0,1:T(8,128)(2,1)} %constant_dynamic-update-slice_fusion, bf16[3072,1536]{1,0:T(8,128)(2,1)} %all-gather.2.cloned.1.call-done), kind=kOutput, calls=%fused_computation.1 | convolution fusion | flops 7248936960 | bytes 16515072 | tf_op jit(solution)/shard_map/dot_general | solution.py:70
  172.6 49.2 %all_to_all.23 = bf16[4,768,384]{2,1,0:T(8,128)(2,1)S(1)} all-to-all(bf16[4,768,384]{2,1,0:T(8,128)(2,1)S(1)} %bitcast.31), channel_id=1, replica_groups=mesh['row'=16,'col'=8,'fiber'=4] {'fiber'}, dimensions={0} | all-to-all | bytes 4718592 | tf_op jit(solution)/shard_map/all_to_all | solution.py:15
  222.9 14.2 %all-to-all-start.3 = ((f32[16,1,384]{2,1,0:T(1,128)}), f32[16,1,384]{2,1,0:T(1,128)}, u32[]{:S(2)}, u32[]{:S(2)}) async-start(f32[16,1,384]{2,1,0:T(1,128)} %broadcast_in_dim.22), calls=%async_computation.3 | async-start | bytes 49152 | tf_op jit(solution)/shard_map/all_to_all | solution.py:21
  238.0 7.3 %all-to-all-done.3 = f32[16,1,384]{2,1,0:T(1,128)} async-done(((f32[16,1,384]{2,1,0:T(1,128)}), f32[16,1,384]{2,1,0:T(1,128)}, u32[]{:S(2)}, u32[]{:S(2)}) %all-to-all-start.3) | async-done | bytes 24608 | tf_op jit(solution)/shard_map/all_to_all | solution.py:21
  246.1 1.1 multiply_divide_fusion
  (29 shorter events, 10.1 us)
Async XLA Ops:
  6.5 154.2 %all-gather.2.cloned.1.call-start = ((), (), s32[]{:S(2)}) async-start(), calls=%async_computation.4 | async-start | bytes 10027008 | tf_op jit(solution)/shard_map/all_gather | solution.py:72
  58.4 15.4 %collective-permute-start = (bf16[768,384]{0,1:T(8,128)(2,1)S(1)}, bf16[768,384]{0,1:T(8,128)(2,1)S(1)}, u32[]{:S(2)}, u32[]{:S(2)}) collective-permute-start(bf16[768,384]{0,1:T(8,128)(2,1)S(1)} %bitcast.38), channel_id=1, source_target_pairs={{0,4},{4,8},{8,12},{12,16},{16,20},{20,24},{24,28},{28,0},{1,5},{5... | collective-permute-start | bytes 1769480 | tf_op jit(solution)/shard_map/ppermute | solution.py:61
  60.5 16.8 %collective-permute-start.1 = (bf16[768,384]{0,1:T(8,128)(2,1)S(1)}, bf16[768,384]{0,1:T(8,128)(2,1)S(1)}, u32[]{:S(2)}, u32[]{:S(2)}) collective-permute-start(bf16[768,384]{0,1:T(8,128)(2,1)S(1)} %bitcast.39), channel_id=1, source_target_pairs={{0,28},{4,0},{8,4},{12,8},{16,12},{20,16},{24,20},{28,24},{1,29},{... | collective-permute-start | bytes 1769480 | tf_op jit(solution)/shard_map/ppermute | solution.py:66
  73.8 14.6 %collective-permute-start.2 = (bf16[768,384]{0,1:T(8,128)(2,1)S(1)}, bf16[768,384]{0,1:T(8,128)(2,1)S(1)}, u32[]{:S(2)}, u32[]{:S(2)}) collective-permute-start(bf16[768,384]{0,1:T(8,128)(2,1)S(1)} %collective-permute-done), channel_id=1, source_target_pairs={{0,4},{4,8},{8,12},{12,16},{16,20},{20,24},{24,28},{28,0},{1,5},{5... | collective-permute-start | bytes 1769480 | tf_op jit(solution)/shard_map/ppermute | solution.py:61
  77.3 19.5 %collective-permute-start.3 = (bf16[768,384]{0,1:T(8,128)(2,1)S(1)}, bf16[768,384]{0,1:T(8,128)(2,1)S(1)}, u32[]{:S(2)}, u32[]{:S(2)}) collective-permute-start(bf16[768,384]{0,1:T(8,128)(2,1)S(1)} %collective-permute-done.1), channel_id=1, source_target_pairs={{0,28},{4,0},{8,4},{12,8},{16,12},{20,16},{24,20},{28,24},{1,29},{... | collective-permute-start | bytes 1769480 | tf_op jit(solution)/shard_map/ppermute | solution.py:66
  88.5 14.3 %collective-permute-start.4 = (bf16[768,384]{0,1:T(8,128)(2,1)S(1)}, bf16[768,384]{0,1:T(8,128)(2,1)S(1)}, u32[]{:S(2)}, u32[]{:S(2)}) collective-permute-start(bf16[768,384]{0,1:T(8,128)(2,1)S(1)} %collective-permute-done.2), channel_id=1, source_target_pairs={{0,4},{4,8},{8,12},{12,16},{16,20},{20,24},{24,28},{28,0},{1,5},{5... | collective-permute-start | bytes 1769480 | tf_op jit(solution)/shard_map/ppermute | solution.py:61
  96.7 15.1 %collective-permute-start.5 = (bf16[768,384]{0,1:T(8,128)(2,1)S(1)}, bf16[768,384]{0,1:T(8,128)(2,1)S(1)}, u32[]{:S(2)}, u32[]{:S(2)}) collective-permute-start(bf16[768,384]{0,1:T(8,128)(2,1)S(1)} %collective-permute-done.3), channel_id=1, source_target_pairs={{0,28},{4,0},{8,4},{12,8},{16,12},{20,16},{24,20},{28,24},{1,29},{... | collective-permute-start | bytes 1769480 | tf_op jit(solution)/shard_map/ppermute | solution.py:66
  102.7 14.3 %collective-permute-start.6 = (bf16[768,384]{0,1:T(8,128)(2,1)S(1)}, bf16[768,384]{0,1:T(8,128)(2,1)S(1)}, u32[]{:S(2)}, u32[]{:S(2)}) collective-permute-start(bf16[768,384]{0,1:T(8,128)(2,1)S(1)} %collective-permute-done.4), channel_id=1, source_target_pairs={{0,4},{4,8},{8,12},{12,16},{16,20},{20,24},{24,28},{28,0},{1,5},{5... | collective-permute-start | bytes 1769480 | tf_op jit(solution)/shard_map/ppermute | solution.py:61
  172.6 64.6 %copy-start = (s32[6,3]{0,1:T(4,128)S(1)}, s32[6,3]{0,1:T(4,128)}, u32[]{:S(2)}) copy-start(s32[6,3]{0,1:T(4,128)} %param.5) | copy-start | bytes 220
  222.9 22.4 %all-to-all-start.3 = ((f32[16,1,384]{2,1,0:T(1,128)}), f32[16,1,384]{2,1,0:T(1,128)}, u32[]{:S(2)}, u32[]{:S(2)}) async-start(f32[16,1,384]{2,1,0:T(1,128)} %broadcast_in_dim.22), calls=%async_computation.3 | async-start | bytes 49152 | tf_op jit(solution)/shard_map/all_to_all | solution.py:21
Sparse Core Ops, SparseCore 0:
  41.1 119.5 all-gather.1
